TPU v7x, 256 devices: a whole 4x4x8 slice. The times are simulated.
256 devices in a mesh: bricks: 64 (over y, z, core), slab: 4 (over x).
Axes of the slice: x: 4, y: 4, z: 8, core: 2. Of those that a mesh axis runs over, the one named last changes fastest.
Arguments:
- part_pos: float32 [256, 3, 2048], P(('bricks', 'slab')), may hold values from 0 to 1, as said below
- part_mass: float32 [256, 2048], P(('bricks', 'slab')), may hold values from 0.5 to 2
- cell_pos: float32 [256, 3, 2048], P(('bricks', 'slab')), may hold values from 0 to 1, as said below
- cell_mass: float32 [256, 2048], P(('bricks', 'slab')), may hold values from 0.5 to 2
- cell_scale: float32 [256, 2048], P(('bricks', 'slab')), may hold values from 0.5 to 2
- req_tile: int32 [16384, 1], P(('bricks', 'slab')), may hold values from 0 to 15, as said below
- tile_bucket: int32 [256, 144], P(('bricks', 'slab')), may hold values from 0 to 15, as said below
- tile_slot: int32 [256, 144], P(('bricks', 'slab')), may hold values from 0 to 63, as said below
- tile_count: int32 [256], P(('bricks', 'slab')), may hold values from 64 to 144, as said below
- lagr_index: int32 [256, 2048], P(('bricks', 'slab')), may hold values from 0 to 2047, each once within a row
Outputs:
- particle_potential: float32 [256, 2048], P(('bricks', 'slab'))
- cell_potential: float32 [256, 2048], P(('bricks', 'slab'))
- divergence: float32 [16, 256, 128], P('slab', 'bricks')
Inputs may be any that keep to these rules, and one draw needn't show every extreme that they name: `part_pos`: device b * 4 + s holds particles of its own brick: component 0 within [0.25 b / 64, 0.25 (b + 1) / 64], component 1 within [0.25 s / 4, 0.25 (s + 1) / 4], component 2 within [0, 1]. `cell_pos`: device b * 4 + s holds the cells of the same brick, bounded as its particles. `req_tile`: over the devices of one slab index, every cell tile of every device is named by exactly four slots. `tile_bucket`: A device's live tiles name each of its buckets at least once. `tile_slot`: A device's live tiles name each of its slots at least once. `tile_count`: the live tiles are the first entries of a device's list; one device has exactly 144, every other between 64 and 80. `lagr_index`: each device's particles fill its block of the Lagrangian grid, one point each.
All inputs are finite; a program needn't handle non-finite values.
Results may differ from a plain program's by a relative error of at most 0.0003.
Values sent between devices are 32-bit elements; how exact they have to be, the bound alone decides.
A program may use at most 64 MiB of HBM per device.

v0:
```python
import jax
import jax.numpy as jnp
from jax import lax
from jax.sharding import PartitionSpec as P

TS = 128
ITERS = 2
LB = 4
EPS = 0.05
tile_group = 16


def with_halo(block, sides, width):
    for axis, dim in sides:
        count = lax.axis_size(axis)
        forward = [(i, i + 1) for i in range(count - 1)]
        backward = [(target, source) for source, target in forward]
        low = lax.ppermute(
            lax.slice_in_dim(block, block.shape[dim] - width, None, axis=dim), axis, forward
        )
        high = lax.ppermute(lax.slice_in_dim(block, 0, width, axis=dim), axis, backward)
        block = jnp.concatenate([low, block, high], axis=dim)
    return block


def tile_kernel(part_tiles, cell_tiles, live_mask):
    distance = (part_tiles[:, 0, :, None] - cell_tiles[:, 0, None, :]) ** 2
    distance = distance + (part_tiles[:, 1, :, None] - cell_tiles[:, 1, None, :]) ** 2
    distance = distance + (part_tiles[:, 2, :, None] - cell_tiles[:, 2, None, :]) ** 2
    return jnp.exp(-distance / EPS) * live_mask[:, None, None]


def grouped(arrays):
    return tuple(
        (
            item.reshape((item.shape[0] // tile_group, tile_group) + item.shape[1:])
            for item in arrays
        )
    )


def row_pass(part_rows, cell_rows, live_mask, buckets, value_rows, bucket_count):

    def row_one_group(pieces):
        part_piece, cell_piece, mask_piece, value_piece = pieces
        kernel = tile_kernel(part_piece, cell_piece, mask_piece)
        return jnp.einsum("tij,tcj->tci", kernel, value_piece, precision=lax.Precision.HIGHEST)

    per_tile = lax.map(row_one_group, grouped((part_rows, cell_rows, live_mask, value_rows)))
    per_tile = per_tile.reshape((-1,) + per_tile.shape[2:])
    one_hot = (buckets[:, None] == jnp.arange(bucket_count, dtype=jnp.int32)[None, :]).astype(
        jnp.float32
    )
    return jnp.einsum("tb,tci->bci", one_hot, per_tile, precision=lax.Precision.HIGHEST)


def column_pass(part_rows, cell_rows, live_mask, slot_ids, scale_rows, slot_total):

    def column_one_group(pieces):
        part_piece, cell_piece, mask_piece, scale_piece = pieces
        kernel = tile_kernel(part_piece, cell_piece, mask_piece)
        return jnp.einsum("tij,ti->tj", kernel, scale_piece, precision=lax.Precision.HIGHEST)

    per_tile = lax.map(column_one_group, grouped((part_rows, cell_rows, live_mask, scale_rows)))
    per_tile = per_tile.reshape((-1,) + per_tile.shape[2:])
    one_hot = (slot_ids[:, None] == jnp.arange(slot_total, dtype=jnp.int32)[None, :]).astype(
        jnp.float32
    )
    return jnp.einsum("ts,tj->sj", one_hot, per_tile, precision=lax.Precision.HIGHEST)


def on_device(
    part_pos,
    part_mass,
    cell_pos,
    cell_mass,
    cell_scale,
    req_tile,
    tile_bucket,
    tile_slot,
    tile_count,
    lagr_index,
):
    places = part_pos[0]
    tile_width = TS
    bucket_count = places.shape[1] // tile_width
    cell_tiles = cell_pos.shape[2] // tile_width
    brick_count = lax.axis_size("bricks")
    per_peer = req_tile.shape[1]
    slot_total = brick_count * per_peer
    part_tiles = places.reshape(3, bucket_count, tile_width).transpose(1, 0, 2)
    own_cells = cell_pos[0].reshape(3, cell_tiles, tile_width).transpose(1, 0, 2)
    buckets = tile_bucket[0]
    slot_ids = tile_slot[0]
    live_mask = (jnp.arange(buckets.shape[0], dtype=jnp.int32) < tile_count[0]).astype(jnp.float32)
    cell_ids = jnp.arange(cell_tiles, dtype=jnp.int32)
    wanted = (jnp.arange(brick_count, dtype=jnp.int32)[:, None] * cell_tiles + req_tile).reshape(
        slot_total
    )
    every_cell = lax.all_gather(own_cells, "bricks", axis=0, tiled=True)
    slot_cells = every_cell[wanted]

    def fetch_duals(values):
        return lax.all_gather(values, "bricks", axis=0, tiled=True)[wanted]

    part_rows = part_tiles[buckets]
    cell_rows = slot_cells[slot_ids]
    masses = part_mass[0].reshape(bucket_count, tile_width)
    cell_masses = cell_mass[0].reshape(cell_tiles, tile_width)
    cell_scaling = cell_scale[0].reshape(cell_tiles, tile_width)
    for sweep in range(ITERS):
        fetched = fetch_duals(cell_scaling[:, None, :])
        totals = row_pass(part_rows, cell_rows, live_mask, buckets, fetched[slot_ids], bucket_count)
        particle_scale = masses / totals[:, 0]
        partial_value = column_pass(
            part_rows, cell_rows, live_mask, slot_ids, particle_scale[buckets], slot_total
        )
        one_hot = (req_tile[:, :, None] == cell_ids[None, None, :]).astype(jnp.float32)
        dense_sums = jnp.einsum(
            "pcq,pct->pqt",
            one_hot,
            partial_value.reshape(brick_count, per_peer, tile_width),
            precision=lax.Precision.HIGHEST,
        )
        cell_scaling = cell_masses / lax.psum_scatter(
            dense_sums.reshape(brick_count * cell_tiles, tile_width),
            "bricks",
            scatter_dimension=0,
            tiled=True,
        )
    weighted = jnp.concatenate(
        [cell_scaling[:, None, :], cell_scaling[:, None, :] * own_cells], axis=1
    )
    fetched = fetch_duals(weighted)
    totals = row_pass(part_rows, cell_rows, live_mask, buckets, fetched[slot_ids], bucket_count)
    particle_scale = masses / totals[:, 0]
    displacement = totals[:, 1:] / totals[:, 0:1] - part_tiles
    displacement = displacement.transpose(1, 0, 2).reshape(3, bucket_count * tile_width)
    lagr_grid = jnp.zeros_like(displacement).at[:, lagr_index[0]].set(displacement)
    planes = lagr_grid.reshape(3, -1, LB, tile_width)
    across = with_halo(planes[0], (("slab", 0),), 1)
    second = with_halo(planes[1], (("bricks", 1),), 1)
    depth_pad = jnp.pad(planes[2], ((0, 0), (0, 0), (1, 1)))
    divergence = 0.5 * (across[2:] - across[:-2])
    divergence = divergence + 0.5 * (second[:, 2:] - second[:, :-2])
    divergence = divergence + 0.5 * (depth_pad[:, :, 2:] - depth_pad[:, :, :-2])
    particle_potential = jnp.log(particle_scale).reshape(1, -1)
    cell_potential = jnp.log(cell_scaling).reshape(1, -1)
    return (particle_potential, cell_potential, divergence)


def solution(mesh):
    return jax.shard_map(
        on_device,
        mesh=mesh,
        in_specs=(
            P(("bricks", "slab"), None, None),
            P(("bricks", "slab"), None),
            P(("bricks", "slab"), None, None),
            P(("bricks", "slab"), None),
            P(("bricks", "slab"), None),
            P(("bricks", "slab"), None),
            P(("bricks", "slab"), None),
            P(("bricks", "slab"), None),
            P(("bricks", "slab")),
            P(("bricks", "slab"), None),
        ),
        out_specs=(
            P(("bricks", "slab"), None),
            P(("bricks", "slab"), None),
            P("slab", "bricks", None),
        ),
        check_vma=False,
    )
```

profile of v0, /device:TPU:14, one launch (start us, length us, event | category | flops | bytes accessed | tf_op | source)
XLA Modules:
  0.0 641.0 jit_solution(7654722147235039259)
XLA Ops:
  11.5 53.0 %all_gather.13 = f32[1024,1,128]{2,0,1:T(8,128)S(1)} all-gather(f32[16,1,128]{2,0,1:T(8,128)} %bitcast.349), channel_id=1, replica_groups=mesh['bricks'=64,'slab'=4] {'bricks'}, dimensions={0}, use_global_device_ids=true | all-gather | bytes 532480 | tf_op jit(solution)/shard_map/all_gather | solution.py:104
  66.6 18.3 %all-gather.4.cloned.1.call-done = f32[1024,3,128]{2,0,1:T(8,128)} async-done(((f32[16,3,128]{2,0,1:T(8,128)}), f32[1024,3,128]{2,0,1:T(8,128)}) %all-gather.4.cloned.1.call-update) | async-done | bytes 1572880 | tf_op jit(solution)/shard_map/all_gather | solution.py:100
  89.1 24.3 %while.50 = (s32[]{:T(128)}, f32[9,16,1,128]{3,2,1,0:T(1,128)S(1)}, f32[9,16,1,128]{3,2,1,0:T(1,128)S(1)}, f32[9,16,3,128]{3,2,1,0:T(4,128)S(1)}, f32[9,16,3,128...) while((s32[]{:T(128)}, f32[9,16,1,128]{3,2,1,0:T(1,128)S(1)}, f32[9,16,1,128]{3,2,1,0:T(1,128)S(1)}, ...), condition=%wide.region_1.2_spmd, body=%wide.region_0.1_spmd.sunk | while | flops 6029314 | bytes 263893 | solution.py:49
  89.2 2.6 fusion.197
  91.9 2.6 fusion.197
  94.6 2.6 fusion.197
  97.3 2.6 fusion.197
  100.0 2.6 fusion.197
  110.8 2.6 fusion.197
  114.3 18.7 %while.51 = (s32[]{:T(128)}, f32[9,16,128]{2,1,0:T(8,128)S(1)}, f32[9,16,3,128]{3,2,1,0:T(4,128)S(1)}, f32[9,16,3,128]{3,2,1,0:T(4,128)S(1)}, f32[9,16]{1,0:T(8,128)S(1)}, /*index=5*/f32[9,16,128]{2,1,0:T(8,128)S(1)}, s32[]{:T(128)}) while((s32[]{:T(128)}, f32[9,16,128]{2,1,0:T(8,128)S(1)}, f32[9,16,3,128]{3,2,1,0:T(4,128)S(1)}, ...), condition=%wide.region_3.4_spmd, body=%wide.region_2.3_spmd.sunk | while | flops 6029314 | bytes 295197 | solution.py:64
  134.4 137.2 %reduce-scatter.3.cloned.1.call-done = f32[16,128]{1,0:T(8,128)} async-done(((f32[1024,128]{1,0:T(8,128)}), f32[16,128]{1,0:T(8,128)}) %reduce-scatter.3.cloned.1.call-update) | async-done | bytes 8208 | tf_op jit(solution)/shard_map/reduce_scatter | solution.py:125
  272.3 48.6 %all-gather = f32[1024,128]{1,0:T(8,128)S(1)} all-gather(f32[16,128]{1,0:T(8,128)S(1)} %div.42), channel_id=2, replica_groups=mesh['bricks'=64,'slab'=4] {'bricks'}, dimensions={0}, use_global_device_ids=true | all-gather | bytes 532480 | tf_op jit(solution)/shard_map/all_gather | solution.py:104
  322.2 24.3 %while.52 = (s32[]{:T(128)}, f32[9,16,1,128]{3,2,1,0:T(1,128)S(1)}, f32[9,16,1,128]{3,2,1,0:T(1,128)S(1)}, f32[9,16,3,128]{3,2,1,0:T(4,128)S(1)}, f32[9,16,3,128...) while((s32[]{:T(128)}, f32[9,16,1,128]{3,2,1,0:T(1,128)S(1)}, f32[9,16,1,128]{3,2,1,0:T(1,128)S(1)}, ...), condition=%wide.region_6.7_spmd, body=%wide.region_5.6_spmd.sunk | while | flops 6029314 | bytes 263893 | solution.py:49
  338.5 2.6 fusion.209
  347.4 18.7 %while.53 = (s32[]{:T(128)}, f32[9,16,128]{2,1,0:T(8,128)S(1)}, f32[9,16,3,128]{3,2,1,0:T(4,128)S(1)}, f32[9,16,3,128]{3,2,1,0:T(4,128)S(1)}, f32[9,16]{1,0:T(8,128)S(1)}, /*index=5*/f32[9,16,128]{2,1,0:T(8,128)S(1)}, s32[]{:T(128)}) while((s32[]{:T(128)}, f32[9,16,128]{2,1,0:T(8,128)S(1)}, f32[9,16,3,128]{3,2,1,0:T(4,128)S(1)}, ...), condition=%wide.region_8.9_spmd, body=%wide.region_7.8_spmd.sunk | while | flops 6029314 | bytes 295197 | solution.py:64
  367.5 138.0 %reduce-scatter.5.cloned.1.call-done = f32[16,128]{1,0:T(8,128)} async-done(((f32[1024,128]{1,0:T(8,128)}), f32[16,128]{1,0:T(8,128)}) %reduce-scatter.5.cloned.1.call-update) | async-done | bytes 8208 | tf_op jit(solution)/shard_map/reduce_scatter | solution.py:125
  507.6 76.2 %all-gather.6.cloned.1.call-done = f32[1024,4,128]{2,1,0:T(4,128)} async-done(((f32[16,4,128]{2,1,0:T(4,128)}), f32[1024,4,128]{2,1,0:T(4,128)}) %all-gather.6.cloned.1.call-update) | async-done | bytes 2097168 | tf_op jit(solution)/shard_map/all_gather | solution.py:104
  586.8 24.2 %while.54 = (s32[]{:T(128)}, f32[9,16,4,128]{3,2,1,0:T(4,128)S(1)}, f32[9,16,4,128]{3,2,1,0:T(4,128)S(1)}, f32[9,16,3,128]{3,1,2,0:T(8,128)S(1)}, f32[9,16,3,128...) while((s32[]{:T(128)}, f32[9,16,4,128]{3,2,1,0:T(4,128)S(1)}, f32[9,16,4,128]{3,2,1,0:T(4,128)S(1)}, ...), condition=%wide.region_11.12_spmd, body=%wide.region_10.11_spmd.sunk | while | flops 15466498 | bytes 313049 | solution.py:49
  594.9 2.6 fusion.219
  605.7 2.6 fusion.219
  611.6 5.8 scatter_custom_fusion
  619.1 4.5 collective-permute-start.2
  625.6 2.8 collective-permute-start
  630.7 3.1 collective-permute-done.1
  (331 shorter events, 113.4 us)
Async XLA Ops:
  7.2 59.3 %copy-start.7 = (s32[64,1]{0,1:T(1,128)S(1)}, s32[64,1]{0,1:T(1,128)}, u32[]{:S(2)}) copy-start(s32[64,1]{0,1:T(1,128)} %param.25) | copy-start | bytes 772
  7.2 77.7 %all-gather.4.cloned.1.call-start = ((), (), s32[]{:S(2)}) async-start(), calls=%async_computation.2 | async-start | bytes 1597440 | tf_op jit(solution)/shard_map/all_gather | solution.py:100
  7.9 263.7 %reduce-scatter.3.cloned.1.call-start = ((), (), s32[]{:S(2)}) async-start(), calls=%async_computation.3 | async-start | bytes 532480 | tf_op jit(solution)/shard_map/reduce_scatter | solution.py:125
  89.0 24.3 %copy-start.2 = (f32[1,2048]{1,0:T(1,128)S(1)}, f32[1,2048]{1,0:T(1,128)}, u32[]{:S(2)}) copy-start(f32[1,2048]{1,0:T(1,128)} %param.21) | copy-start | bytes 24580
  89.1 24.3 %copy-start.4 = (s32[1,144]{1,0:T(1,128)S(1)}, s32[1,144]{1,0:T(1,128)}, u32[]{:S(2)}) copy-start(s32[1,144]{1,0:T(1,128)} %param.26) | copy-start | bytes 1732
  114.3 18.7 %copy-start.5 = (s32[1,144]{1,0:T(1,128)S(1)}, s32[1,144]{1,0:T(1,128)}, u32[]{:S(2)}) copy-start(s32[1,144]{1,0:T(1,128)} %param.27) | copy-start | bytes 1732
  114.3 157.4 %copy-start.3 = (f32[1,2048]{1,0:T(1,128)S(1)}, f32[1,2048]{1,0:T(1,128)}, u32[]{:S(2)}) copy-start(f32[1,2048]{1,0:T(1,128)} %param.23) | copy-start | bytes 24580
  134.4 371.2 %reduce-scatter.5.cloned.1.call-start = ((), (), s32[]{:S(2)}) async-start(), calls=%async_computation.4 | async-start | bytes 532480 | tf_op jit(solution)/shard_map/reduce_scatter | solution.py:125
  347.4 159.5 %copy-start = (f32[1,3,2048]{2,0,1:T(1,128)S(1)}, f32[1,3,2048]{2,0,1:T(1,128)}, u32[]{:S(2)}) copy-start(f32[1,3,2048]{2,0,1:T(1,128)} %param.22) | copy-start | bytes 73732
  347.4 160.1 %copy-start.6 = (s32[1,2048]{1,0:T(1,128)S(1)}, s32[1,2048]{1,0:T(1,128)}, u32[]{:S(2)}) copy-start(s32[1,2048]{1,0:T(1,128)} %param.29) | copy-start | bytes 24580
  367.5 216.2 %all-gather.6.cloned.1.call-start = ((), (), s32[]{:S(2)}) async-start(), calls=%async_computation.5 | async-start | bytes 2129920 | tf_op jit(solution)/shard_map/all_gather | solution.py:104
  586.8 24.4 %copy-start.1 = (f32[1,3,2048]{2,0,1:T(1,128)S(1)}, f32[1,3,2048]{2,0,1:T(1,128)}, u32[]{:S(2)}) copy-start(f32[1,3,2048]{2,0,1:T(1,128)} %param.20) | copy-start | bytes 73732
  619.1 11.2 %collective-permute-start.2 = (f32[4,1,128]{2,1,0:T(1,128)S(1)}, f32[4,1,128]{2,1,0:T(1,128)S(1)}, u32[]{:S(2)}, u32[]{:S(2)}) collective-permute-start(f32[4,1,128]{2,1,0:T(1,128)S(1)} %get-tuple-element.398), channel_id=1, source_target_pairs={{4,0},{8,4},{12,8},{16,12},{20,16},{24,20},{28,24},{32,28},{36,32}... | collective-permute-start | bytes 6152 | tf_op jit(solution)/shard_map/ppermute | solution.py:21
  623.6 7.0 %collective-permute-start.3 = (f32[4,1,128]{2,1,0:T(1,128)S(1)}, f32[4,1,128]{2,1,0:T(1,128)S(1)}, u32[]{:S(2)}, u32[]{:S(2)}) collective-permute-start(f32[4,1,128]{2,1,0:T(1,128)S(1)} %get-tuple-element.399), channel_id=1, source_target_pairs={{0,4},{4,8},{8,12},{12,16},{16,20},{20,24},{24,28},{28,32},{32,36}... | collective-permute-start | bytes 6152 | tf_op jit(solution)/shard_map/ppermute | solution.py:18
  625.6 5.1 collective-permute-start
  628.3 5.5 collective-permute-start.1
Sparse Core Ops, SparseCore 0:
  10.6 74.3 all-gather.3
  134.5 137.1 reduce-scatter.2
  367.6 137.8 reduce-scatter.4
  508.2 75.5 all-gather.5
where the time goes:
time: 642 us; the launch traced here: 641 us
  waiting for transfers between devices  374 us (58%)
  matrix products  106 us (17%)
  blocking collectives  102 us (16%)
  local copies, waits for them, and re-layouts  24.4 us (4%)
  between operations  14.7 us (2%)
  starting transfers between devices  10.7 us (2%)
  other arithmetic  7.51 us (1%)
    reduce_scatter x2, waiting for transfers between devices, on_device(): lax.psum_scatter(dense_sums.reshape(brick_count * cell_tiles, tile_width)...  275 us
    all_gather x2, blocking collectives, fetch_duals(): return lax.all_gather(values, 'bricks', axis=0, tiled=True)[wanted]  102 us
    all_gather x1, waiting for transfers between devices, fetch_duals(): return lax.all_gather(values, 'bricks', axis=0, tiled=True)[wanted]  76.2 us
    dot_general x27, matrix products, row_one_group(): jnp.einsum('tij,tcj->tci', kernel, value_piece, precision=lax.Precision.H...  70 us
    dot_general x18, matrix products, column_one_group(): jnp.einsum('tij,ti->tj', kernel, scale_piece, precision=lax.Precision.HIG...  35 us
    all_gather x1, waiting for transfers between devices, on_device(): every_cell = lax.all_gather(own_cells, 'bricks', axis=0, tiled=True)  18.3 us
  transfers between devices with their start and end apart: 8, of which 6 were waited for; matrix products, arithmetic and copies ran while one was open for 1% of the time, Pallas kernels for 0%

commit v1 on v0

--- a/solution.py
+++ b/solution.py
@@ -8,6 +8,18 @@
 LB = 4
 EPS = 0.05
 tile_group = 16
+
+
+def collect(x, axis, dim):
+    ways, here, step = (lax.axis_size(axis), lax.axis_index(axis), x.shape[dim])
+    line, have = (x, 1)
+    while have < ways:
+        line = jnp.concatenate(
+            [line, lax.ppermute(line, axis, [(d, (d - have) % ways) for d in range(ways)])],
+            axis=dim,
+        )
+        have = 2 * have
+    return jnp.roll(line, here * step, axis=dim)
 
 
 def with_halo(block, sides, width):
@@ -101,7 +113,7 @@
     slot_cells = every_cell[wanted]
 
     def fetch_duals(values):
-        return lax.all_gather(values, "bricks", axis=0, tiled=True)[wanted]
+        return collect(values, "bricks", 0)[wanted]
 
     part_rows = part_tiles[buckets]
     cell_rows = slot_cells[slot_ids]

time: 642 us -> 640 us (level)
  blocking collectives: 102 us -> 0 us
  starting transfers between devices: 10.7 us -> 73 us
  waiting for transfers between devices: 374 us -> 396 us
  local copies, waits for them, and re-layouts: 24.4 us -> 36.9 us
    all_gather x2 -> x0, blocking collectives: 102 us -> none  [fetch_duals(): return lax.all_gather(values, 'bricks', axis=0, tiled=True)[wanted]]
    all_gather x1 -> x0, waiting for transfers between devices: 76.2 us -> none  [fetch_duals(): return lax.all_gather(values, 'bricks', axis=0, tiled=True)[wanted]]
    ppermute x0 -> x18, waiting for transfers between devices: none -> 75.3 us  [collect(): lax.ppermute(line, axis, [(d, (d - have) % ways) for d in range(ways)])]
    ppermute x0 -> x18, starting transfers between devices: none -> 52.7 us  [collect(): lax.ppermute(line, axis, [(d, (d - have) % ways) for d in range(ways)])]
    all_gather x1, waiting for transfers between devices: 18.3 us -> 34.3 us  [on_device(): every_cell = lax.all_gather(own_cells, 'bricks', axis=0, tiled=True)]
    ppermute x2, starting transfers between devices: 7.29 us -> 16.9 us  [with_halo(): lax.ppermute(lax.slice_in_dim(block, 0, width, axis=dim), axis, backward)]
    unnamed x16 -> x36, local copies, waits for them, and re-layouts: 0.06 us -> 9.48 us
    reduce_scatter x2, waiting for transfers between devices: 275 us -> 282 us  [on_device(): lax.psum_scatter(dense_sums.reshape(brick_count * cell_tiles, tile_width)...]
  transfers between devices with their start and end apart: 8 -> 25, of which waited for: 6 -> 22; matrix products, arithmetic and copies ran while one was open for 1% -> 2% of each run, Pallas kernels for 0% -> 0%
where the time goes in v1:
time: 640 us
  waiting for transfers between devices  396 us (62%)
  matrix products  106 us (17%)
  starting transfers between devices  73 us (11%)
  local copies, waits for them, and re-layouts  36.9 us (6%)
  between operations  14.8 us (2%)
  other arithmetic  11 us (2%)
    reduce_scatter x2, waiting for transfers between devices, on_device(): lax.psum_scatter(dense_sums.reshape(brick_count * cell_tiles, tile_width)...  282 us
    ppermute x18, waiting for transfers between devices, collect(): lax.ppermute(line, axis, [(d, (d - have) % ways) for d in range(ways)])  75.3 us
    dot_general x27, matrix products, row_one_group(): jnp.einsum('tij,tcj->tci', kernel, value_piece, precision=lax.Precision.H...  70 us
    ppermute x18, starting transfers between devices, collect(): lax.ppermute(line, axis, [(d, (d - have) % ways) for d in range(ways)])  52.7 us
    dot_general x18, matrix products, column_one_group(): jnp.einsum('tij,ti->tj', kernel, scale_piece, precision=lax.Precision.HIG...  35 us
    all_gather x1, waiting for transfers between devices, on_device(): every_cell = lax.all_gather(own_cells, 'bricks', axis=0, tiled=True)  34.3 us
    ppermute x2, starting transfers between devices, with_halo(): lax.ppermute(lax.slice_in_dim(block, 0, width, axis=dim), axis, backward)  16.9 us
  transfers between devices with their start and end apart: 25, of which 22 were waited for; matrix products, arithmetic and copies ran while one was open for 2% of the time, Pallas kernels for 0%

profile of v1, /device:TPU:14, one launch (start us, length us, event | category | flops | bytes accessed | tf_op | source)
XLA Modules:
  0.0 639.5 jit_solution(7219246684619159528)
XLA Ops:
  8.6 5.3 collective-permute-start
  22.6 3.5 collective-permute-done.2
  28.8 6.3 collective-permute-done.3
  35.1 3.4 collective-permute-start.4
  51.3 34.3 %all-gather.2.cloned.1.call-done = f32[1024,3,128]{2,0,1:T(8,128)} async-done(((f32[16,3,128]{2,0,1:T(8,128)}), f32[1024,3,128]{2,0,1:T(8,128)}) %all-gather.2.cloned.1.call-update) | async-done | bytes 1572880 | tf_op jit(solution)/shard_map/all_gather | solution.py:112
  89.8 24.3 %while.50 = (s32[]{:T(128)}, f32[9,16,1,128]{3,2,1,0:T(1,128)S(1)}, f32[9,16,1,128]{3,2,1,0:T(1,128)S(1)}, f32[9,16,3,128]{3,2,1,0:T(4,128)S(1)}, f32[9,16,3,128...) while((s32[]{:T(128)}, f32[9,16,1,128]{3,2,1,0:T(1,128)S(1)}, f32[9,16,1,128]{3,2,1,0:T(1,128)S(1)}, ...), condition=%wide.region_1.3_spmd, body=%wide.region_0.2_spmd.sunk | while | flops 6029314 | bytes 263893 | solution.py:61
  115.0 18.7 %while.51 = (s32[]{:T(128)}, f32[9,16,128]{2,1,0:T(8,128)S(1)}, f32[9,16,3,128]{3,2,1,0:T(4,128)S(1)}, f32[9,16,3,128]{3,2,1,0:T(4,128)S(1)}, f32[9,16]{1,0:T(8,128)S(1)}, /*index=5*/f32[9,16,128]{2,1,0:T(8,128)S(1)}, s32[]{:T(128)}) while((s32[]{:T(128)}, f32[9,16,128]{2,1,0:T(8,128)S(1)}, f32[9,16,3,128]{3,2,1,0:T(4,128)S(1)}, ...), condition=%wide.region_3.5_spmd, body=%wide.region_2.4_spmd.sunk | while | flops 6029314 | bytes 295197 | solution.py:76
  135.1 137.3 %reduce-scatter.3.cloned.1.call-done = f32[16,128]{1,0:T(8,128)} async-done(((f32[1024,128]{1,0:T(8,128)}), f32[16,128]{1,0:T(8,128)}) %reduce-scatter.3.cloned.1.call-update) | async-done | bytes 8208 | tf_op jit(solution)/shard_map/reduce_scatter | solution.py:137
  283.5 5.1 collective-permute-start.9
  296.9 3.4 collective-permute-start.11
  300.3 5.0 collective-permute-done.11
  306.9 24.3 %while.52 = (s32[]{:T(128)}, f32[9,16,1,128]{3,2,1,0:T(1,128)S(1)}, f32[9,16,1,128]{3,2,1,0:T(1,128)S(1)}, f32[9,16,3,128]{3,2,1,0:T(4,128)S(1)}, f32[9,16,3,128...) while((s32[]{:T(128)}, f32[9,16,1,128]{3,2,1,0:T(1,128)S(1)}, f32[9,16,1,128]{3,2,1,0:T(1,128)S(1)}, ...), condition=%wide.region_6.8_spmd, body=%wide.region_5.7_spmd.sunk | while | flops 6029314 | bytes 263893 | solution.py:61
  332.1 18.7 %while.53 = (s32[]{:T(128)}, f32[9,16,128]{2,1,0:T(8,128)S(1)}, f32[9,16,3,128]{3,2,1,0:T(4,128)S(1)}, f32[9,16,3,128]{3,2,1,0:T(4,128)S(1)}, f32[9,16]{1,0:T(8,128)S(1)}, /*index=5*/f32[9,16,128]{2,1,0:T(8,128)S(1)}, s32[]{:T(128)}) while((s32[]{:T(128)}, f32[9,16,128]{2,1,0:T(8,128)S(1)}, f32[9,16,3,128]{3,2,1,0:T(4,128)S(1)}, ...), condition=%wide.region_8.10_spmd, body=%wide.region_7.9_spmd.sunk | while | flops 6029314 | bytes 295197 | solution.py:76
  352.2 145.1 %reduce-scatter.5.cloned.1.call-done = f32[16,128]{1,0:T(8,128)} async-done(((f32[1024,128]{1,0:T(8,128)}), f32[16,128]{1,0:T(8,128)}) %reduce-scatter.5.cloned.1.call-update) | async-done | bytes 8208 | tf_op jit(solution)/shard_map/reduce_scatter | solution.py:137
  509.5 4.6 collective-permute-done.14
  514.1 4.9 collective-permute-start.15
  521.0 6.5 %collective-permute-done.15 = f32[128,4,128]{2,1,0:T(4,128)S(1)} collective-permute-done((f32[128,4,128]{2,1,0:T(4,128)S(1)}, f32[128,4,128]{2,1,0:T(4,128)S(1)}, u32[]{:S(2)}, u32[]{:S(2)}) %collective-permute-start.15) | collective-permute-done | bytes 262176 | tf_op jit(solution)/shard_map/ppermute | solution.py:18
  528.5 8.0 %collective-permute-start.16 = (f32[256,4,128]{2,1,0:T(4,128)S(1)}, f32[256,4,128]{2,1,0:T(4,128)S(1)}, u32[]{:S(2)}, u32[]{:S(2)}) collective-permute-start(f32[256,4,128]{2,1,0:T(4,128)S(1)} %get-tuple-element.405), channel_id=1, source_target_pairs={{0,192},{4,196},{8,200},{12,204},{16,208},{20,212},{24,216},{28,22... | collective-permute-start | bytes 1572872 | tf_op jit(solution)/shard_map/ppermute | solution.py:18
  536.4 7.7 %collective-permute-done.16 = f32[256,4,128]{2,1,0:T(4,128)S(1)} collective-permute-done((f32[256,4,128]{2,1,0:T(4,128)S(1)}, f32[256,4,128]{2,1,0:T(4,128)S(1)}, u32[]{:S(2)}, u32[]{:S(2)}) %collective-permute-start.16) | collective-permute-done | bytes 524320 | tf_op jit(solution)/shard_map/ppermute | solution.py:18
  547.2 19.1 %collective-permute-done.17 = f32[512,4,128]{2,1,0:T(4,128)S(1)} collective-permute-done((f32[512,4,128]{2,1,0:T(4,128)}, f32[512,4,128]{2,1,0:T(4,128)S(1)}, u32[]{:S(2)}, u32[]{:S(2)}) %collective-permute-start.17) | collective-permute-done | bytes 1048608 | tf_op jit(solution)/shard_map/ppermute | solution.py:18
  575.6 24.2 %while.54 = (s32[]{:T(128)}, f32[9,16,4,128]{3,2,1,0:T(4,128)S(1)}, f32[9,16,4,128]{3,2,1,0:T(4,128)S(1)}, f32[9,16,3,128]{3,1,2,0:T(8,128)S(1)}, f32[9,16,3,128...) while((s32[]{:T(128)}, f32[9,16,4,128]{3,2,1,0:T(4,128)S(1)}, f32[9,16,4,128]{3,2,1,0:T(4,128)S(1)}, ...), condition=%wide.region_11.13_spmd, body=%wide.region_10.12_spmd.sunk | while | flops 15466498 | bytes 313049 | solution.py:61
  600.4 5.8 scatter_custom_fusion
  607.9 14.0 %collective-permute-start.20 = (f32[4,1,128]{2,1,0:T(1,128)S(1)}, f32[4,1,128]{2,1,0:T(1,128)S(1)}, u32[]{:S(2)}, u32[]{:S(2)}) collective-permute-start(f32[4,1,128]{2,1,0:T(1,128)S(1)} %get-tuple-element.441), channel_id=1, source_target_pairs={{4,0},{8,4},{12,8},{16,12},{20,16},{24,20},{28,24},{32,28},{36,32}... | collective-permute-start | bytes 6152 | tf_op jit(solution)/shard_map/ppermute | solution.py:33
  629.0 3.3 collective-permute-done.19
  (400 shorter events, 200.2 us)
Async XLA Ops:
  7.2 78.4 %all-gather.2.cloned.1.call-start = ((), (), s32[]{:S(2)}) async-start(), calls=%async_computation.2 | async-start | bytes 1597440 | tf_op jit(solution)/shard_map/all_gather | solution.py:112
  8.6 263.9 %reduce-scatter.3.cloned.1.call-start = ((), (), s32[]{:S(2)}) async-start(), calls=%async_computation.3 | async-start | bytes 532480 | tf_op jit(solution)/shard_map/reduce_scatter | solution.py:137
  8.6 7.4 %collective-permute-start = (f32[16,1,128]{2,0,1:T(8,128)}, f32[16,1,128]{2,0,1:T(8,128)S(1)}, u32[]{:S(2)}, u32[]{:S(2)}) collective-permute-start(f32[16,1,128]{2,0,1:T(8,128)} %bitcast.341), channel_id=1, source_target_pairs={{0,252},{4,0},{8,4},{12,8},{16,12},{20,16},{24,20},{28,24},{32,28}... | collective-permute-start | bytes 24584 | tf_op jit(solution)/shard_map/ppermute | solution.py:18
  16.7 3.7 collective-permute-start.1
  21.2 5.0 collective-permute-start.2
  26.9 8.2 %collective-permute-start.3 = (f32[128,1,128]{2,0,1:T(8,128)S(1)}, f32[128,1,128]{2,0,1:T(8,128)S(1)}, u32[]{:S(2)}, u32[]{:S(2)}) collective-permute-start(f32[128,1,128]{2,0,1:T(8,128)S(1)} %pad_maximum_fusion.2), channel_id=1, source_target_pairs={{0,224},{4,228},{8,232},{12,236},{16,240},{20,244},{24,248},{28,25... | collective-permute-start | bytes 196616 | tf_op jit(solution)/shard_map/ppermute | solution.py:18
  35.1 6.0 collective-permute-start.4
  41.1 8.5 %collective-permute-start.5 = (f32[512,1,128]{2,0,1:T(8,128)S(1)}, f32[512,1,128]{2,0,1:T(8,128)S(1)}, u32[]{:S(2)}, u32[]{:S(2)}) collective-permute-start(f32[512,1,128]{2,0,1:T(8,128)S(1)} %get-tuple-element.411), channel_id=1, source_target_pairs={{0,128},{4,132},{8,136},{12,140},{16,144},{20,148},{24,152},{28,15... | collective-permute-start | bytes 786440 | tf_op jit(solution)/shard_map/ppermute | solution.py:18
  135.1 362.3 %reduce-scatter.5.cloned.1.call-start = ((), (), s32[]{:S(2)}) async-start(), calls=%async_computation.4 | async-start | bytes 532480 | tf_op jit(solution)/shard_map/reduce_scatter | solution.py:137
  274.5 4.2 collective-permute-start.7
  278.7 4.8 collective-permute-start.8
  283.5 8.3 %collective-permute-start.9 = (f32[128,1,128]{2,0,1:T(8,128)S(1)}, f32[128,1,128]{2,0,1:T(8,128)S(1)}, u32[]{:S(2)}, u32[]{:S(2)}) collective-permute-start(f32[128,1,128]{2,0,1:T(8,128)S(1)} %pad_maximum_fusion.3), channel_id=1, source_target_pairs={{0,224},{4,228},{8,232},{12,236},{16,240},{20,244},{24,248},{28,25... | collective-permute-start | bytes 196616 | tf_op jit(solution)/shard_map/ppermute | solution.py:18
  291.8 5.0 collective-permute-start.10
  296.9 8.4 %collective-permute-start.11 = (f32[512,1,128]{2,0,1:T(8,128)S(1)}, f32[512,1,128]{2,0,1:T(8,128)S(1)}, u32[]{:S(2)}, u32[]{:S(2)}) collective-permute-start(f32[512,1,128]{2,0,1:T(8,128)S(1)} %get-tuple-element.409), channel_id=1, source_target_pairs={{0,128},{4,132},{8,136},{12,140},{16,144},{20,148},{24,152},{28,15... | collective-permute-start | bytes 786440 | tf_op jit(solution)/shard_map/ppermute | solution.py:18
  499.3 1.6 collective-permute-start.12
  500.9 5.0 collective-permute-start.13
  506.0 8.1 %collective-permute-start.14 = (f32[64,4,128]{2,1,0:T(4,128)S(1)}, f32[64,4,128]{2,1,0:T(4,128)S(1)}, u32[]{:S(2)}, u32[]{:S(2)}) collective-permute-start(f32[64,4,128]{2,1,0:T(4,128)S(1)} %pad_maximum_fusion.1), channel_id=1, source_target_pairs={{0,240},{4,244},{8,248},{12,252},{16,0},{20,4},{24,8},{28,12},{32,... | collective-permute-start | bytes 393224 | tf_op jit(solution)/shard_map/ppermute | solution.py:18
  514.1 13.4 %collective-permute-start.15 = (f32[128,4,128]{2,1,0:T(4,128)S(1)}, f32[128,4,128]{2,1,0:T(4,128)S(1)}, u32[]{:S(2)}, u32[]{:S(2)}) collective-permute-start(f32[128,4,128]{2,1,0:T(4,128)S(1)} %pad_maximum_fusion), channel_id=1, source_target_pairs={{0,224},{4,228},{8,232},{12,236},{16,240},{20,244},{24,248},{28,25... | collective-permute-start | bytes 786440 | tf_op jit(solution)/shard_map/ppermute | solution.py:18
  528.5 15.7 %collective-permute-start.16 = (f32[256,4,128]{2,1,0:T(4,128)S(1)}, f32[256,4,128]{2,1,0:T(4,128)S(1)}, u32[]{:S(2)}, u32[]{:S(2)}) collective-permute-start(f32[256,4,128]{2,1,0:T(4,128)S(1)} %get-tuple-element.405), channel_id=1, source_target_pairs={{0,192},{4,196},{8,200},{12,204},{16,208},{20,212},{24,216},{28,22... | collective-permute-start | bytes 1572872 | tf_op jit(solution)/shard_map/ppermute | solution.py:18
  545.2 21.1 %collective-permute-start.17 = (f32[512,4,128]{2,1,0:T(4,128)}, f32[512,4,128]{2,1,0:T(4,128)S(1)}, u32[]{:S(2)}, u32[]{:S(2)}) collective-permute-start(f32[512,4,128]{2,1,0:T(4,128)} %get-tuple-element.401), channel_id=1, source_target_pairs={{0,128},{4,132},{8,136},{12,140},{16,144},{20,148},{24,152},{28,15... | collective-permute-start | bytes 3145736 | tf_op jit(solution)/shard_map/ppermute | solution.py:18
  607.9 20.8 %collective-permute-start.20 = (f32[4,1,128]{2,1,0:T(1,128)S(1)}, f32[4,1,128]{2,1,0:T(1,128)S(1)}, u32[]{:S(2)}, u32[]{:S(2)}) collective-permute-start(f32[4,1,128]{2,1,0:T(1,128)S(1)} %get-tuple-element.441), channel_id=1, source_target_pairs={{4,0},{8,4},{12,8},{16,12},{20,16},{24,20},{28,24},{32,28},{36,32}... | collective-permute-start | bytes 6152 | tf_op jit(solution)/shard_map/ppermute | solution.py:33
  622.0 7.0 %collective-permute-start.21 = (f32[4,1,128]{2,1,0:T(1,128)S(1)}, f32[4,1,128]{2,1,0:T(1,128)S(1)}, u32[]{:S(2)}, u32[]{:S(2)}) collective-permute-start(f32[4,1,128]{2,1,0:T(1,128)S(1)} %get-tuple-element.442), channel_id=1, source_target_pairs={{0,4},{4,8},{8,12},{12,16},{16,20},{20,24},{24,28},{28,32},{32,36}... | collective-permute-start | bytes 6152 | tf_op jit(solution)/shard_map/ppermute | solution.py:30
  623.9 5.1 collective-permute-start.18
  626.8 5.5 collective-permute-start.19
  (8 other events, 613.6 us)
Sparse Core Ops, SparseCore 0:
  10.5 75.0 all-gather.1
  135.2 137.2 reduce-scatter.2
  352.3 144.9 reduce-scatter.4
